TPU v7x, 128 devices: a whole 4x4x4 slice. The times are simulated.
128 devices in a mesh: row: 8 (over x, y_hi), col: 16 (over y_lo, z, core).
Axes of the slice: x: 4, y: 4 (y_hi: 2, y_lo: 2; y = y_hi * 2 + y_lo), z: 4, core: 2. Of those that a mesh axis runs over, the one named last changes fastest.
Arguments:
- coupling: bfloat16 [32768, 32768], P('row', 'col'), may hold values from -0.03125 to 0.03125
- amplitude: float32 [64, 32768], P(None, 'col'), may hold values from -0.95 to 0.95
- target: float32 [64, 32768], P(None, 'col'), may hold values from -6 to 6
- shadow_target: float32 [64, 32768], P(None, 'col'), may hold values from -10.2 to 10.2
Outputs:
- solution: float32 [64, 32768], P(None, 'col')
- shadow_solution: float32 [64, 32768], P(None, 'col')
- residual: float32 [64, 32768], P(None, 'col')
- shadow_residual: float32 [64, 32768], P(None, 'col')
All inputs are finite; a program needn't handle non-finite values.
Results may differ from a plain program's by a relative error of at most 0.0036.
Values may be sent and summed in bfloat16 or wider, within the bound.
No kernel may reach another device: no remote copies, remote signals or barrier semaphores. Data moves between devices by JAX's collectives and lax.ppermute only.
A program may use at most 128 MiB of HBM per device.

v0:
```python
import jax
import jax.numpy as jnp
from jax import lax
from jax.sharding import PartitionSpec as P

ITERS = 2
SELF_GAIN = 0.5
COUPLE_GAIN = 0.3


def on_device(coupling, amplitude, target, shadow_target):
    row_rows = coupling.shape[0]
    col_rows = coupling.shape[1]
    row_index = lax.axis_index("row")
    col_index = lax.axis_index("col")
    slope = 1.0 - amplitude * amplitude
    solution = jnp.zeros_like(target)
    shadow_solution = jnp.zeros_like(target)
    residual = target
    shadow_residual = shadow_target
    direction = target
    shadow_direction = shadow_target
    align = lax.psum(jnp.sum(shadow_residual * residual, axis=1), "col")
    for iteration in range(ITERS):
        scaled = (slope * direction).astype(jnp.bfloat16)
        primary_gathered = lax.all_gather(scaled, "col", axis=1, tiled=True)
        row_block = lax.dynamic_slice_in_dim(primary_gathered, row_index * row_rows, row_rows, 1)
        primary_partial_value = jnp.dot(row_block, coupling, preferred_element_type=jnp.float32)
        product = lax.psum(primary_partial_value, "row")
        image = direction - SELF_GAIN * slope * direction - COUPLE_GAIN * product
        shadow_scaled = shadow_direction.astype(jnp.bfloat16)
        partial_value = lax.dot_general(
            shadow_scaled, coupling, (((1,), (1,)), ((), ())), preferred_element_type=jnp.float32
        )
        summed = lax.psum(partial_value, "col")
        gathered = lax.all_gather(summed, "row", axis=1, tiled=True)
        own_block = lax.dynamic_slice_in_dim(gathered, col_index * col_rows, col_rows, 1)
        shadow_image = (
            shadow_direction
            - SELF_GAIN * slope * shadow_direction
            - COUPLE_GAIN * slope * own_block
        )
        curve = lax.psum(jnp.sum(shadow_direction * image, axis=1), "col")
        step_size = align / curve
        column_step = step_size[:, None]
        solution = solution + column_step * direction
        shadow_solution = shadow_solution + column_step * shadow_direction
        residual = residual - column_step * image
        shadow_residual = shadow_residual - column_step * shadow_image
        if iteration + 1 < ITERS:
            align_next = lax.psum(jnp.sum(shadow_residual * residual, axis=1), "col")
        if iteration + 1 < ITERS:
            blend = (align_next / align)[:, None]
            direction = residual + blend * direction
            shadow_direction = shadow_residual + blend * shadow_direction
            align = align_next
    return (solution, shadow_solution, residual, shadow_residual)


def solution(mesh):
    return jax.shard_map(
        on_device,
        mesh=mesh,
        in_specs=(P("row", "col"), P(None, "col"), P(None, "col"), P(None, "col")),
        out_specs=(P(None, "col"), P(None, "col"), P(None, "col"), P(None, "col")),
        check_vma=False,
    )
```

profile of v0, /device:TPU:1, one launch (start us, length us, event | category | flops | bytes accessed | tf_op | source)
XLA Modules:
  0.0 766.5 jit_solution(14258358741011477803)
XLA Ops:
  7.2 0.0 all-gather.5.cloned.1.call-start
  7.2 2.1 multiply_convert_fusion.1
  9.3 0.0 all-gather.5.cloned.1.call-update
  9.3 0.0 all-reduce.8.cloned.1.call-start
  9.4 12.1 %fusion.14 = f32[64,4096]{1,0:T(8,128)} fusion(bf16[4096,2048]{1,0:T(8,128)(2,1)} %param.4, f32[64,2048]{1,0:T(8,128)} %param.7), kind=kOutput, calls=%fused_computation.31 | convolution fusion | flops 1073872896 | bytes 18350080 | tf_op jit(solution)/shard_map/dot_general | solution.py:32
  21.5 0.0 copy-start
  21.5 0.0 copy-start.1
  21.5 0.0 copy-start.2
  21.5 0.0 all-reduce.8.cloned.1.call-update
  21.5 0.0 all-reduce.6.cloned.1.call-start
  21.6 29.8 %all-gather.5.cloned.1.call-done = bf16[64,32768]{1,0:T(8,128)(2,1)} async-done(((bf16[64,2048]{1,0:T(8,128)(2,1)}), bf16[64,32768]{1,0:T(8,128)(2,1)}) %all-gather.5.cloned.1.call-update) | async-done | bytes 4194320 | tf_op jit(solution)/shard_map/all_gather | solution.py:26
  51.3 9.8 %fusion.10 = f32[64,2048]{1,0:T(8,128)} fusion(bf16[4096,2048]{1,0:T(8,128)(2,1)} %param.4, bf16[64,32768]{1,0:T(8,128)(2,1)} %all-gather.5.cloned.1.call-done, s32[]{:T(128)S(6)} %select_n.8), kind=kOutput, calls=%fused_computation.24 | convolution fusion | flops 1073741824 | bytes 17825796 | tf_op jit(solution)/shard_map/dot_general | solution.py:28
  61.1 0.0 all-reduce.6.cloned.1.call-update
  61.1 0.0 all-gather.7.cloned.1.call-start
  61.2 111.6 %all-reduce.8.cloned.1.call-done = f32[64,4096]{1,0:T(8,128)} async-done(((f32[64,4096]{1,0:T(8,128)}), f32[64,4096]{1,0:T(8,128)}) %all-reduce.8.cloned.1.call-update) | async-done | bytes 1048592 | tf_op jit(solution)/shard_map/psum | solution.py:35
  172.8 0.0 all-gather.7.cloned.1.call-update
  172.8 0.0 all-gather.9.cloned.1.call-start
  172.9 84.5 %all-reduce.6.cloned.1.call-done = f32[64,2048]{1,0:T(8,128)} async-done(((f32[64,2048]{1,0:T(8,128)}), f32[64,2048]{1,0:T(8,128)}) %all-reduce.6.cloned.1.call-update) | async-done | bytes 524304 | tf_op jit(solution)/shard_map/psum | solution.py:29
  257.3 0.0 copy-done
  257.3 0.0 copy-done.1
  257.3 0.0 copy-done.2
  257.3 1.3 multiply_reduce_fusion.2
  258.7 32.6 %all-reduce = (f32[64]{0:T(128)S(1)}, f32[64]{0:T(128)S(1)}) all-reduce(f32[64]{0:T(128)S(1)} %get-tuple-element.5, f32[64]{0:T(128)S(1)} %get-tuple-element.4), channel_id=1, replica_groups=mesh['row'=8,'col'=16] {'col'}, use_global_device_ids=true, to_apply=%region_1.0 | all-reduce | flops 128 | bytes 1024 | tf_op jit(solution)/shard_map/psum | solution.py:23
  291.3 79.8 %all-gather.7.cloned.1.call-done = f32[64,32768]{1,0:T(8,128)} async-done(((f32[64,4096]{1,0:T(8,128)}), f32[64,32768]{1,0:T(8,128)}) %all-gather.7.cloned.1.call-update) | async-done | bytes 8388624 | tf_op jit(solution)/shard_map/all_gather | solution.py:36
  371.0 1.6 multiply_reduce_fusion.1
  372.7 27.6 %psum.60 = f32[64]{0:T(128)S(1)} all-reduce(f32[64]{0:T(128)S(1)} %get-tuple-element.10), channel_id=1, replica_groups=mesh['row'=8,'col'=16] {'col'}, use_global_device_ids=true, to_apply=%region_7.0 | all-reduce | flops 64 | bytes 512 | tf_op jit(solution)/shard_map/psum | solution.py:51
  400.3 0.9 multiply_convert_fusion
  401.1 0.0 all-gather.9.cloned.1.call-update
  401.1 0.0 all-reduce.12.cloned.1.call-start
  401.2 12.0 %fusion.12 = f32[64,4096]{1,0:T(8,128)} fusion(bf16[4096,2048]{1,0:T(8,128)(2,1)} %param.4, f32[64,2048]{1,0:T(8,128)S(1)} %get-tuple-element.12, f32[64,2048]{1,0:T(8,128)S(1)} %copy-done, f32[64]{0:T(128)S(1)} %div.10), kind=kOutput, calls=%fused_computation.29 | convolution fusion | flops 1074135040 | bytes 18874624 | tf_op jit(solution)/shard_map/dot_general | solution.py:32
  413.2 0.0 all-reduce.12.cloned.1.call-update
  413.2 0.2 all-reduce.10.cloned.1.call-start
  413.4 23.9 %all-gather.9.cloned.1.call-done = bf16[64,32768]{1,0:T(8,128)(2,1)} async-done(((bf16[64,2048]{1,0:T(8,128)(2,1)}), bf16[64,32768]{1,0:T(8,128)(2,1)}) %all-gather.9.cloned.1.call-update) | async-done | bytes 4194320 | tf_op jit(solution)/shard_map/all_gather | solution.py:26
  437.4 9.8 %fusion.8 = f32[64,2048]{1,0:T(8,128)} fusion(bf16[4096,2048]{1,0:T(8,128)(2,1)} %param.4, bf16[64,32768]{1,0:T(8,128)(2,1)} %all-gather.9.cloned.1.call-done, s32[]{:T(128)S(6)} %select_n.8), kind=kOutput, calls=%fused_computation.16 | convolution fusion | flops 1073741824 | bytes 17825796 | tf_op jit(solution)/shard_map/dot_general | solution.py:28
  447.1 0.0 all-reduce.10.cloned.1.call-update
  447.1 0.0 all-gather.11.cloned.1.call-start
  447.2 111.4 %all-reduce.12.cloned.1.call-done = f32[64,4096]{1,0:T(8,128)} async-done(((f32[64,4096]{1,0:T(8,128)}), f32[64,4096]{1,0:T(8,128)}) %all-reduce.12.cloned.1.call-update) | async-done | bytes 1048592 | tf_op jit(solution)/shard_map/psum | solution.py:35
  558.6 0.0 all-gather.11.cloned.1.call-update
  558.7 84.5 %all-reduce.10.cloned.1.call-done = f32[64,2048]{1,0:T(8,128)} async-done(((f32[64,2048]{1,0:T(8,128)}), f32[64,2048]{1,0:T(8,128)}) %all-reduce.10.cloned.1.call-update) | async-done | bytes 524304 | tf_op jit(solution)/shard_map/psum | solution.py:29
  643.2 1.4 multiply_reduce_fusion
  644.6 32.6 %psum.62 = f32[64]{0:T(128)S(1)} all-reduce(f32[64]{0:T(128)S(1)} %get-tuple-element.8), channel_id=1, replica_groups=mesh['row'=8,'col'=16] {'col'}, use_global_device_ids=true, to_apply=%region_10.0 | all-reduce | flops 64 | bytes 512 | tf_op jit(solution)/shard_map/psum | solution.py:43
  677.2 79.8 %all-gather.11.cloned.1.call-done = f32[64,32768]{1,0:T(8,128)} async-done(((f32[64,4096]{1,0:T(8,128)}), f32[64,32768]{1,0:T(8,128)}) %all-gather.11.cloned.1.call-update) | async-done | bytes 8388624 | tf_op jit(solution)/shard_map/all_gather | solution.py:36
  757.0 2.7 multiply_subtract_fusion.4
  (3 shorter events, 0.0 us)
Async XLA Ops:
  7.2 44.2 %all-gather.5.cloned.1.call-start = ((), (), s32[]{:S(2)}) async-start(), calls=%async_computation | async-start | bytes 4456448 | tf_op jit(solution)/shard_map/all_gather | solution.py:26
  9.3 163.5 %all-reduce.8.cloned.1.call-start = ((), (), s32[]{:S(2)}) async-start(), calls=%async_computation.2 | async-start | bytes 2097152 | tf_op jit(solution)/shard_map/psum | solution.py:35
  21.5 235.8 %copy-start = (f32[64,2048]{1,0:T(8,128)S(1)}, f32[64,2048]{1,0:T(8,128)}, u32[]{:S(2)}) copy-start(f32[64,2048]{1,0:T(8,128)} %param.7) | copy-start | bytes 1572868
  21.5 235.8 %copy-start.1 = (f32[64,2048]{1,0:T(8,128)S(1)}, f32[64,2048]{1,0:T(8,128)}, u32[]{:S(2)}) copy-start(f32[64,2048]{1,0:T(8,128)} %param.6) | copy-start | bytes 1572868
  21.5 235.8 %copy-start.2 = (f32[64,2048]{1,0:T(8,128)S(1)}, f32[64,2048]{1,0:T(8,128)}, u32[]{:S(2)}) copy-start(f32[64,2048]{1,0:T(8,128)} %param.5) | copy-start | bytes 1572868
  21.5 235.8 %all-reduce.6.cloned.1.call-start = ((), (), s32[]{:S(2)}) async-start(), calls=%async_computation.1 | async-start | bytes 1048576 | tf_op jit(solution)/shard_map/psum | solution.py:29
  61.1 309.9 %all-gather.7.cloned.1.call-start = ((), (), s32[]{:S(2)}) async-start(), calls=%async_computation.3 | async-start | bytes 9437184 | tf_op jit(solution)/shard_map/all_gather | solution.py:36
  172.8 264.5 %all-gather.9.cloned.1.call-start = ((), (), s32[]{:S(2)}) async-start(), calls=%async_computation.4 | async-start | bytes 4456448 | tf_op jit(solution)/shard_map/all_gather | solution.py:26
  401.1 157.5 %all-reduce.12.cloned.1.call-start = ((), (), s32[]{:S(2)}) async-start(), calls=%async_computation.6 | async-start | bytes 2097152 | tf_op jit(solution)/shard_map/psum | solution.py:35
  413.2 230.0 %all-reduce.10.cloned.1.call-start = ((), (), s32[]{:S(2)}) async-start(), calls=%async_computation.5 | async-start | bytes 1048576 | tf_op jit(solution)/shard_map/psum | solution.py:29
  447.1 309.9 %all-gather.11.cloned.1.call-start = ((), (), s32[]{:S(2)}) async-start(), calls=%async_computation.7 | async-start | bytes 9437184 | tf_op jit(solution)/shard_map/all_gather | solution.py:36
Sparse Core Ops, SparseCore 0:
  10.2 41.0 all-gather.4
  53.8 118.9 all-reduce.7
  176.0 81.2 all-reduce.5
  259.5 111.4 all-gather.6
  401.2 36.0 all-gather.8
  439.7 118.9 all-reduce.11
  561.9 81.2 all-reduce.9
  645.5 111.4 all-gather.10
where the time goes:
time: 767 us
  waiting for transfers between devices  605 us (79%)
  blocking collectives  92.8 us (12%)
  matrix products  43.6 us (6%)
  between operations  14.2 us (2%)
  other arithmetic  10 us (1%)
    psum x2, waiting for transfers between devices, on_device(): summed = lax.psum(partial_value, 'col')  223 us
    psum x2, waiting for transfers between devices, on_device(): product = lax.psum(primary_partial_value, 'row')  169 us
    all_gather x2, waiting for transfers between devices, on_device(): gathered = lax.all_gather(summed, 'row', axis=1, tiled=True)  160 us
    all_gather x2, waiting for transfers between devices, on_device(): primary_gathered = lax.all_gather(scaled, 'col', axis=1, tiled=True)  53.7 us
    psum x1, blocking collectives, on_device(): curve = lax.psum(jnp.sum(shadow_direction * image, axis=1), 'col')  32.6 us
    psum x1, blocking collectives, on_device(): align = lax.psum(jnp.sum(shadow_residual * residual, axis=1), 'col')  32.6 us
    psum x1, blocking collectives, on_device(): align_next = lax.psum(jnp.sum(shadow_residual * residual, axis=1), 'col')  27.6 us
    dot_general x2, matrix products, on_device(): lax.dot_general(shadow_scaled, coupling, (((1,), (1,)), ((), ())), prefer...  24.1 us
  transfers between devices with their start and end apart: 8, of which 8 were waited for; matrix products, arithmetic and copies ran while one was open for 6% of the time, Pallas kernels for 0%

commit v1 on v0

--- a/solution.py
+++ b/solution.py
@@ -26,7 +26,7 @@
         primary_gathered = lax.all_gather(scaled, "col", axis=1, tiled=True)
         row_block = lax.dynamic_slice_in_dim(primary_gathered, row_index * row_rows, row_rows, 1)
         primary_partial_value = jnp.dot(row_block, coupling, preferred_element_type=jnp.float32)
-        product = lax.psum(primary_partial_value, "row")
+        product = jnp.sum(lax.all_gather(primary_partial_value, "row"), axis=0)
         image = direction - SELF_GAIN * slope * direction - COUPLE_GAIN * product
         shadow_scaled = shadow_direction.astype(jnp.bfloat16)
         partial_value = lax.dot_general(

time: 767 us -> 739 us (0.963)
  waiting for transfers between devices: 605 us -> 584 us
  blocking collectives: 92.8 us -> 83 us
    psum x2 -> x0, waiting for transfers between devices: 169 us -> none  [on_device(): product = lax.psum(primary_partial_value, 'row')]
    all_gather x0 -> x2, waiting for transfers between devices: none -> 150 us  [on_device(): product = jnp.sum(lax.all_gather(primary_partial_value, 'row'), axis=0)]
  transfers between devices with their start and end apart: 8 -> 8, of which waited for: 8 -> 8; matrix products, arithmetic and copies ran while one was open for 6% -> 7% of each run, Pallas kernels for 0% -> 0%
where the time goes in v1:
time: 739 us
  waiting for transfers between devices  584 us (79%)
  blocking collectives  83 us (11%)
  matrix products  43.6 us (6%)
  between operations  14.2 us (2%)
  other arithmetic  13.6 us (2%)
    psum x2, waiting for transfers between devices, on_device(): summed = lax.psum(partial_value, 'col')  223 us
    all_gather x2, waiting for transfers between devices, on_device(): gathered = lax.all_gather(summed, 'row', axis=1, tiled=True)  156 us
    all_gather x2, waiting for transfers between devices, on_device(): product = jnp.sum(lax.all_gather(primary_partial_value, 'row'), axis=0)  150 us
    all_gather x2, waiting for transfers between devices, on_device(): primary_gathered = lax.all_gather(scaled, 'col', axis=1, tiled=True)  53.8 us
    psum x1, blocking collectives, on_device(): curve = lax.psum(jnp.sum(shadow_direction * image, axis=1), 'col')  27.7 us
    psum x1, blocking collectives, on_device(): align = lax.psum(jnp.sum(shadow_residual * residual, axis=1), 'col')  27.7 us
    psum x1, blocking collectives, on_device(): align_next = lax.psum(jnp.sum(shadow_residual * residual, axis=1), 'col')  27.6 us
    dot_general x2, matrix products, on_device(): lax.dot_general(shadow_scaled, coupling, (((1,), (1,)), ((), ())), prefer...  24.1 us
  transfers between devices with their start and end apart: 8, of which 8 were waited for; matrix products, arithmetic and copies ran while one was open for 7% of the time, Pallas kernels for 0%

profile of v1, /device:TPU:1, one launch (start us, length us, event | category | flops | bytes accessed | tf_op | source)
XLA Modules:
  0.0 739.0 jit_solution(13784505021746393224)
XLA Ops:
  7.2 0.0 all-gather.9.cloned.1.call-start
  7.2 2.0 multiply_convert_fusion.1
  9.2 0.0 all-gather.9.cloned.1.call-update
  9.2 0.0 all-reduce.4.cloned.1.call-start
  9.3 12.1 %fusion.14 = f32[64,4096]{1,0:T(8,128)} fusion(bf16[4096,2048]{1,0:T(8,128)(2,1)} %param.4, f32[64,2048]{1,0:T(8,128)} %param.7), kind=kOutput, calls=%fused_computation.31 | convolution fusion | flops 1073872896 | bytes 18350080 | tf_op jit(solution)/shard_map/dot_general | solution.py:32
  21.4 0.0 copy-start
  21.4 0.0 copy-start.1
  21.4 0.0 copy-start.2
  21.4 0.0 all-reduce.4.cloned.1.call-update
  21.4 0.0 all-gather.17.cloned.1.call-start
  21.4 29.9 %all-gather.9.cloned.1.call-done = bf16[64,32768]{1,0:T(8,128)(2,1)} async-done(((bf16[64,2048]{1,0:T(8,128)(2,1)}), bf16[64,32768]{1,0:T(8,128)(2,1)}) %all-gather.9.cloned.1.call-update) | async-done | bytes 4194320 | tf_op jit(solution)/shard_map/all_gather | solution.py:26
  51.4 9.8 %fusion.10 = f32[64,2048]{1,0:T(8,128)} fusion(bf16[4096,2048]{1,0:T(8,128)(2,1)} %param.4, bf16[64,32768]{1,0:T(8,128)(2,1)} %all-gather.9.cloned.1.call-done, s32[]{:T(128)S(6)} %select_n.8), kind=kOutput, calls=%fused_computation.24 | convolution fusion | flops 1073741824 | bytes 17825796 | tf_op jit(solution)/shard_map/dot_general | solution.py:28
  61.1 0.0 all-gather.17.cloned.1.call-update
  61.1 0.0 all-gather.11.cloned.1.call-start
  61.2 111.6 %all-reduce.4.cloned.1.call-done = f32[64,4096]{1,0:T(8,128)} async-done(((f32[64,4096]{1,0:T(8,128)}), f32[64,4096]{1,0:T(8,128)}) %all-reduce.4.cloned.1.call-update) | async-done | bytes 1048592 | tf_op jit(solution)/shard_map/psum | solution.py:35
  172.8 0.0 all-gather.11.cloned.1.call-update
  172.8 0.0 all-gather.13.cloned.1.call-start
  172.9 75.3 %all-gather.17.cloned.1.call-done = f32[512,2048]{1,0:T(8,128)} async-done(((f32[64,2048]{1,0:T(8,128)}), f32[512,2048]{1,0:T(8,128)}) %all-gather.17.cloned.1.call-update) | async-done | bytes 4194320 | tf_op jit(solution)/shard_map/all_gather | solution.py:29
  248.2 2.5 reduce_sum.55
  250.7 0.0 copy-done
  250.7 0.0 copy-done.1
  250.7 0.0 copy-done.2
  250.7 0.3 multiply_reduce_fusion.2
  251.0 27.7 %all-reduce = (f32[64]{0:T(128)S(1)}, f32[64]{0:T(128)S(1)}) all-reduce(f32[64]{0:T(128)S(1)} %get-tuple-element.5, f32[64]{0:T(128)S(1)} %get-tuple-element.4), channel_id=1, replica_groups=mesh['row'=8,'col'=16] {'col'}, use_global_device_ids=true, to_apply=%region_1.0 | all-reduce | flops 128 | bytes 1024 | tf_op jit(solution)/shard_map/psum | solution.py:23
  278.7 78.7 %all-gather.11.cloned.1.call-done = f32[64,32768]{1,0:T(8,128)} async-done(((f32[64,4096]{1,0:T(8,128)}), f32[64,32768]{1,0:T(8,128)}) %all-gather.11.cloned.1.call-update) | async-done | bytes 8388624 | tf_op jit(solution)/shard_map/all_gather | solution.py:36
  357.4 1.5 multiply_reduce_fusion.1
  358.9 27.6 %psum.45 = f32[64]{0:T(128)S(1)} all-reduce(f32[64]{0:T(128)S(1)} %get-tuple-element.10), channel_id=1, replica_groups=mesh['row'=8,'col'=16] {'col'}, use_global_device_ids=true, to_apply=%region_7.0 | all-reduce | flops 64 | bytes 512 | tf_op jit(solution)/shard_map/psum | solution.py:51
  386.5 0.9 multiply_convert_fusion
  387.3 0.0 all-gather.13.cloned.1.call-update
  387.4 0.0 all-reduce.6.cloned.1.call-start
  387.4 12.0 %fusion.12 = f32[64,4096]{1,0:T(8,128)} fusion(bf16[4096,2048]{1,0:T(8,128)(2,1)} %param.4, f32[64,2048]{1,0:T(8,128)S(1)} %get-tuple-element.12, f32[64,2048]{1,0:T(8,128)S(1)} %copy-done, f32[64]{0:T(128)S(1)} %div.10), kind=kOutput, calls=%fused_computation.29 | convolution fusion | flops 1074135040 | bytes 18874624 | tf_op jit(solution)/shard_map/dot_general | solution.py:32
  399.4 0.0 all-reduce.6.cloned.1.call-update
  399.4 0.2 all-gather.19.cloned.1.call-start
  399.7 23.9 %all-gather.13.cloned.1.call-done = bf16[64,32768]{1,0:T(8,128)(2,1)} async-done(((bf16[64,2048]{1,0:T(8,128)(2,1)}), bf16[64,32768]{1,0:T(8,128)(2,1)}) %all-gather.13.cloned.1.call-update) | async-done | bytes 4194320 | tf_op jit(solution)/shard_map/all_gather | solution.py:26
  423.6 9.8 %fusion.8 = f32[64,2048]{1,0:T(8,128)} fusion(bf16[4096,2048]{1,0:T(8,128)(2,1)} %param.4, bf16[64,32768]{1,0:T(8,128)(2,1)} %all-gather.13.cloned.1.call-done, s32[]{:T(128)S(6)} %select_n.8), kind=kOutput, calls=%fused_computation.16 | convolution fusion | flops 1073741824 | bytes 17825796 | tf_op jit(solution)/shard_map/dot_general | solution.py:28
  433.4 0.0 all-gather.19.cloned.1.call-update
  433.4 0.0 all-gather.15.cloned.1.call-start
  433.4 111.6 %all-reduce.6.cloned.1.call-done = f32[64,4096]{1,0:T(8,128)} async-done(((f32[64,4096]{1,0:T(8,128)}), f32[64,4096]{1,0:T(8,128)}) %all-reduce.6.cloned.1.call-update) | async-done | bytes 1048592 | tf_op jit(solution)/shard_map/psum | solution.py:35
  545.1 0.0 all-gather.15.cloned.1.call-update
  545.1 75.1 %all-gather.19.cloned.1.call-done = f32[512,2048]{1,0:T(8,128)} async-done(((f32[64,2048]{1,0:T(8,128)}), f32[512,2048]{1,0:T(8,128)}) %all-gather.19.cloned.1.call-update) | async-done | bytes 4194320 | tf_op jit(solution)/shard_map/all_gather | solution.py:29
  620.2 2.5 reduce_sum.58
  622.6 1.2 multiply_reduce_fusion
  623.8 27.7 %psum.46 = f32[64]{0:T(128)S(1)} all-reduce(f32[64]{0:T(128)S(1)} %get-tuple-element.8), channel_id=1, replica_groups=mesh['row'=8,'col'=16] {'col'}, use_global_device_ids=true, to_apply=%region_10.0 | all-reduce | flops 64 | bytes 512 | tf_op jit(solution)/shard_map/psum | solution.py:43
  651.6 77.7 %all-gather.15.cloned.1.call-done = f32[64,32768]{1,0:T(8,128)} async-done(((f32[64,4096]{1,0:T(8,128)}), f32[64,32768]{1,0:T(8,128)}) %all-gather.15.cloned.1.call-update) | async-done | bytes 8388624 | tf_op jit(solution)/shard_map/all_gather | solution.py:36
  729.3 2.8 multiply_subtract_fusion.4
  (3 shorter events, 0.0 us)
Async XLA Ops:
  7.2 44.2 %all-gather.9.cloned.1.call-start = ((), (), s32[]{:S(2)}) async-start(), calls=%async_computation | async-start | bytes 4456448 | tf_op jit(solution)/shard_map/all_gather | solution.py:26
  9.2 163.6 %all-reduce.4.cloned.1.call-start = ((), (), s32[]{:S(2)}) async-start(), calls=%async_computation.1 | async-start | bytes 2097152 | tf_op jit(solution)/shard_map/psum | solution.py:35
  21.4 229.3 %copy-start = (f32[64,2048]{1,0:T(8,128)S(1)}, f32[64,2048]{1,0:T(8,128)}, u32[]{:S(2)}) copy-start(f32[64,2048]{1,0:T(8,128)} %param.7) | copy-start | bytes 1572868
  21.4 229.3 %copy-start.1 = (f32[64,2048]{1,0:T(8,128)S(1)}, f32[64,2048]{1,0:T(8,128)}, u32[]{:S(2)}) copy-start(f32[64,2048]{1,0:T(8,128)} %param.6) | copy-start | bytes 1572868
  21.4 229.3 %copy-start.2 = (f32[64,2048]{1,0:T(8,128)S(1)}, f32[64,2048]{1,0:T(8,128)}, u32[]{:S(2)}) copy-start(f32[64,2048]{1,0:T(8,128)} %param.5) | copy-start | bytes 1572868
  21.4 226.8 %all-gather.17.cloned.1.call-start = ((), (), s32[]{:S(2)}) async-start(), calls=%async_computation.6 | async-start | bytes 4718592 | tf_op jit(solution)/shard_map/all_gather | solution.py:29
  61.1 296.3 %all-gather.11.cloned.1.call-start = ((), (), s32[]{:S(2)}) async-start(), calls=%async_computation.2 | async-start | bytes 9437184 | tf_op jit(solution)/shard_map/all_gather | solution.py:36
  172.8 250.8 %all-gather.13.cloned.1.call-start = ((), (), s32[]{:S(2)}) async-start(), calls=%async_computation.3 | async-start | bytes 4456448 | tf_op jit(solution)/shard_map/all_gather | solution.py:26
  387.4 157.7 %all-reduce.6.cloned.1.call-start = ((), (), s32[]{:S(2)}) async-start(), calls=%async_computation.4 | async-start | bytes 2097152 | tf_op jit(solution)/shard_map/psum | solution.py:35
  399.4 220.7 %all-gather.19.cloned.1.call-start = ((), (), s32[]{:S(2)}) async-start(), calls=%async_computation.7 | async-start | bytes 4718592 | tf_op jit(solution)/shard_map/all_gather | solution.py:29
  433.4 295.9 %all-gather.15.cloned.1.call-start = ((), (), s32[]{:S(2)}) async-start(), calls=%async_computation.5 | async-start | bytes 9437184 | tf_op jit(solution)/shard_map/all_gather | solution.py:36
Sparse Core Ops, SparseCore 0:
  10.2 41.0 all-gather.8
  53.8 118.9 all-reduce.3
  176.0 72.1 all-gather.16
  250.7 106.7 all-gather.10
  387.5 36.0 all-gather.12
  426.1 118.9 all-reduce.5
  548.0 72.1 all-gather.18
  622.5 106.7 all-gather.14
